TPU v7x, 32 devices: a whole 2x2x4 slice. The times are simulated.
32 devices in a mesh: groups: 2 (over x), gx: 16 (over z, y, core).
Axes of the slice: x: 2, y: 2, z: 4, core: 2. Of those that a mesh axis runs over, the one named last changes fastest.
Arguments:
- hidden_state: bfloat16 [320, 18432], P('groups', 'gx'), parts along dimension 0, may hold values from -80 to 80
- norm_gain: float32 [18432], P('gx'), may hold values from 0.1 to 1.9
- query_weight: bfloat16 [18432, 8192], P(None, 'gx'), may hold values from -0.046875 to 0.046875
- keyval_weight: bfloat16 [18432, 512], P('gx'), may hold values from -0.046875 to 0.046875
- out_weight: bfloat16 [8192, 18432], P('gx'), may hold values from -0.25 to 0.25
- cache_entries: bfloat16 [320, 512, 512], P(('groups', 'gx')), parts along dimension 0, may hold values from -400 to 400
- cache_lengths: int32 [320], P(('groups', 'gx')), parts along dimension 0, may hold values from 2 to 511, as said below
Outputs:
- layer_out: bfloat16 [320, 18432], P('groups', 'gx'), parts along dimension 0
There are 2 independent parts, one for each index of `groups`. A program takes and returns all parts, laid end to end along the dimension named above; an argument that names none is the same for every part. Nothing has to cross between parts.
Inputs may be any that keep to these rules, and one draw needn't show every extreme that they name: `cache_lengths`: slots at or beyond a row's length hold entries that must be ignored.
All inputs are finite; a program needn't handle non-finite values.
Results may differ from a plain program's by a relative error of at most 0.012.
Values may be sent and summed in bfloat16 or wider, within the bound.
A program may use at most 128 MiB of HBM per device.

v0:
```python
import jax
import jax.numpy as jnp
from jax import lax
from jax.sharding import PartitionSpec as P


def on_device(
    hidden_state, norm_gain, query_weight, keyval_weight, out_weight, cache_entries, cache_lengths
):
    members = lax.axis_size("gx")
    rows_all = hidden_state.shape[0]
    width_local = hidden_state.shape[1]
    width = width_local * members
    rows_local = rows_all // members
    head_size = keyval_weight.shape[1] // 2
    state32 = hidden_state.astype(jnp.float32)
    row_total, row_squares = lax.psum(
        (jnp.sum(state32, axis=1), jnp.sum(state32 * state32, axis=1)), "gx"
    )
    row_mean = row_total / width
    row_var = row_squares / width - row_mean * row_mean
    normed_local = (
        (state32 - row_mean[:, None]) * lax.rsqrt(row_var + 1e-05)[:, None] * norm_gain
    ).astype(jnp.bfloat16)
    query_sum = jnp.dot(
        lax.all_gather(normed_local, "gx", axis=1, tiled=True),
        query_weight,
        preferred_element_type=jnp.float32,
    )
    query = (query_sum * head_size ** (-0.5)).astype(jnp.bfloat16)
    new_entry = lax.psum_scatter(
        jnp.dot(normed_local, keyval_weight, preferred_element_type=jnp.float32).astype(
            jnp.bfloat16
        ),
        "gx",
        scatter_dimension=0,
        tiled=True,
    )
    query_rows = lax.all_to_all(query, "gx", split_axis=0, concat_axis=1, tiled=True)
    heads_all = query_rows.shape[1] // head_size
    query3 = query_rows.reshape(rows_local, heads_all, head_size)
    keys = cache_entries[:, :, :head_size]
    values = cache_entries[:, :, head_size:]
    scores = jnp.einsum("rhd,rld->rhl", query3, keys, preferred_element_type=jnp.float32)
    fresh = jnp.einsum(
        "rhd,rd->rh", query3, new_entry[:, :head_size], preferred_element_type=jnp.float32
    )
    valid = jnp.arange(keys.shape[1])[None, :] < cache_lengths[:, None]
    scores = jnp.where(valid[:, None, :], scores, -1e30)
    peak = jnp.maximum(jnp.max(scores, axis=-1), fresh)
    weights = jnp.exp(scores - peak[..., None]) * valid[:, None, :].astype(jnp.float32)
    fresh_w = jnp.exp(fresh - peak)
    total = jnp.sum(weights, axis=-1) + fresh_w
    probs = (weights / total[..., None]).astype(jnp.bfloat16)
    fresh_p = (fresh_w / total).astype(jnp.bfloat16)
    mixed = jnp.einsum("rhl,rld->rhd", probs, values, preferred_element_type=jnp.float32)
    mixed = mixed + fresh_p.astype(jnp.float32)[..., None] * new_entry[:, None, head_size:].astype(
        jnp.float32
    )
    attended_rows = mixed.reshape(rows_local, heads_all * head_size).astype(jnp.bfloat16)
    attended = lax.all_to_all(attended_rows, "gx", split_axis=1, concat_axis=0, tiled=True)
    partial_out = jnp.dot(attended, out_weight, preferred_element_type=jnp.float32)
    summed = lax.psum_scatter(
        partial_out.astype(jnp.bfloat16), "gx", scatter_dimension=1, tiled=True
    ).astype(jnp.float32)
    return (hidden_state.astype(jnp.float32) + summed).astype(jnp.bfloat16)


def solution(mesh):
    in_specs = (
        P("groups", "gx"),
        P("gx"),
        P(None, "gx"),
        P("gx", None),
        P("gx", None),
        P(("groups", "gx"), None, None),
        P(("groups", "gx")),
    )
    out_specs = P("groups", "gx")
    return jax.shard_map(
        on_device, mesh=mesh, in_specs=in_specs, out_specs=out_specs, check_vma=False
    )
```

profile of v0, /device:TPU:0, one launch (start us, length us, event | category | flops | bytes accessed | tf_op | source)
XLA Modules:
  0.0 356.3 jit_solution(5723958601429073780)
XLA Ops:
  6.5 1.3 convert_reduce_fusion
  7.8 34.9 %all-reduce.1 = (f32[160]{0:T(256)S(1)}, f32[160]{0:T(256)S(1)}) all-reduce(f32[160]{0:T(256)S(1)} %get-tuple-element.6, f32[160]{0:T(256)S(1)} %get-tuple-element.5), channel_id=1, replica_groups=mesh['groups'=2,'gx'=16] {'gx'}, use_global_device_ids=true, to_apply=%region_3.0 | all-reduce | flops 320 | bytes 2560 | tf_op jit(solution)/shard_map/psum | solution.py:17
  42.7 2.0 fusion.16
  44.8 2.0 convolution_convert_fusion.1
  46.9 54.8 %all-gather.2.cloned.1.call-done = bf16[160,18432]{1,0:T(8,128)(2,1)} async-done(((bf16[160,1152]{1,0:T(8,128)(2,1)}), bf16[160,18432]{1,0:T(8,128)(2,1)}) %all-gather.2.cloned.1.call-update) | async-done | bytes 5898256 | tf_op jit(solution)/shard_map/all_gather | solution.py:26
  101.7 11.3 %fusion.10 = bf16[160,512]{1,0:T(8,128)(2,1)S(1)} fusion(bf16[160,18432]{1,0:T(8,128)(2,1)} %all-gather.2.cloned.1.call-done, bf16[18432,512]{1,0:T(8,128)(2,1)} %param.9), kind=kOutput, calls=%fused_computation.12 | convolution fusion | flops 3020062720 | bytes 24936448 | tf_op jit(solution)/shard_map/dot_general | solution.py:25
  113.1 0.8 all_to_all.24
  113.8 3.5 all-to-all-start
  117.4 0.1 fusion.28
  117.5 0.6 dynamic-slice
  118.8 74.0 %all-reduce.4.cloned.1.call-done = bf16[160,512]{1,0:T(8,128)(2,1)} async-done(((bf16[160,512]{1,0:T(8,128)(2,1)}), bf16[160,512]{1,0:T(8,128)(2,1)}) %all-reduce.4.cloned.1.call-update) | async-done | bytes 163856
  192.8 0.8 dynamic-slice_convert_fusion
  193.6 0.1 copy.11
  193.8 0.1 fusion.23
  193.9 2.7 fusion.29
  196.6 0.3 fusion.19
  196.9 2.3 fusion.11
  199.3 0.1 copy.12
  199.4 15.5 %all_to_all.32 = bf16[10,16,512]{2,0,1:T(8,128)(2,1)S(1)} all-to-all(bf16[10,16,512]{2,0,1:T(8,128)(2,1)S(1)} %copy.12), channel_id=1, replica_groups=mesh['groups'=2,'gx'=16] {'gx'}, dimensions={1} | all-to-all | bytes 327680 | tf_op jit(solution)/shard_map/all_to_all | solution.py:61
  215.0 12.2 %convolution_convert_fusion = bf16[160,18432]{1,0:T(8,128)(2,1)} fusion(bf16[160,512]{1,0:T(8,128)(2,1)S(1)} %all_to_all.29, bf16[512,18432]{1,0:T(8,128)(2,1)} %param.11), kind=kOutput, calls=%fused_computation | convolution fusion | flops 3022848000 | bytes 24936448 | tf_op jit(solution)/shard_map/dot_general | solution.py:62
  227.2 10.6 %copy.15 = bf16[160,18432]{0,1:T(8,128)(2,1)} copy(bf16[160,18432]{1,0:T(8,128)(2,1)} %convolution_convert_fusion) | data formatting | bytes 11796480
  237.9 109.8 %reduce-scatter.4.cloned.1.call-done = bf16[1152,160]{1,0:T(8,128)(2,1)} async-done(((bf16[18432,160]{1,0:T(8,128)(2,1)}), bf16[1152,160]{1,0:T(8,128)(2,1)}) %reduce-scatter.4.cloned.1.call-update) | async-done | bytes 368656
  347.6 1.3 copy.16
  348.9 0.8 fusion.18
  (23 shorter events, 0.4 us)
Async XLA Ops:
  6.5 38.3 %copy-start = (bf16[1152,512]{1,0:T(8,128)(2,1)S(1)}, bf16[1152,512]{1,0:T(8,128)(2,1)}, u32[]{:S(2)}) copy-start(bf16[1152,512]{1,0:T(8,128)(2,1)} %param.10) | copy-start | bytes 3538948
  6.5 95.2 %all-gather.2.cloned.1.call-start = ((), (), s32[]{:S(2)}) async-start(), calls=%async_computation.3 | async-start | bytes 6266880 | tf_op jit(solution)/shard_map/all_gather | solution.py:26
  44.8 148.0 %all-reduce.4.cloned.1.call-start = ((), (), s32[]{:S(2)}) async-start(), calls=%async_computation.5 | async-start | bytes 327680
  46.9 70.5 %copy-start.3 = (s32[10]{0:T(128)S(1)}, s32[10]{0:T(128)}, u32[]{:S(2)}) copy-start(s32[10]{0:T(128)} %param.13) | copy-start | bytes 124
  46.9 70.6 %copy-start.4 = (u32[32]{0:T(128)S(1)}, u32[32]{0:T(128)}, u32[]{:S(2)}) copy-start(u32[32]{0:T(128)} %constant.18) | copy-start | bytes 388
  113.8 79.8 %all-to-all-start = ((bf16[16,10,512]{2,1,0:T(8,128)(2,1)}), bf16[16,10,512]{2,1,0:T(8,128)(2,1)S(1)}, u32[]{:S(2)}, u32[]{:S(2)}) async-start(bf16[16,10,512]{2,1,0:T(8,128)(2,1)} %all_to_all.24), calls=%async_computation | async-start | bytes 524288 | tf_op jit(solution)/shard_map/all_to_all | solution.py:39
  117.4 230.3 %reduce-scatter.4.cloned.1.call-start = ((), (), s32[]{:S(2)}) async-start(), calls=%async_computation.4 | async-start | bytes 10027008
  227.2 122.6 %copy-start.1 = (bf16[1152,512]{1,0:T(8,128)(2,1)S(1)}, bf16[1152,512]{1,0:T(8,128)(2,1)}, u32[]{:S(2)}) copy-start(bf16[1152,512]{1,0:T(8,128)(2,1)} %param.10) | copy-start | bytes 3538948
  237.8 111.1 %copy-start.2 = (bf16[160,1152]{1,0:T(8,128)(2,1)S(1)}, bf16[160,1152]{1,0:T(8,128)(2,1)}, u32[]{:S(2)}) copy-start(bf16[160,1152]{1,0:T(8,128)(2,1)} %param.7) | copy-start | bytes 1105924
Sparse Core Ops, SparseCore 0:
  44.9 56.8 all-gather.1
  105.2 87.5 all-reduce.3
  238.0 109.5 reduce-scatter.3
where the time goes:
time: 357 us; the launch traced here: 356 us
  waiting for transfers between devices  239 us (67%)
  blocking collectives  50.4 us (14%)
  matrix products  30.8 us (9%)
  between operations  13.9 us (4%)
  local copies, waits for them, and re-layouts  13.7 us (4%)
  other arithmetic  5.25 us (1%)
  starting transfers between devices  3.62 us (1%)
    unnamed x5, waiting for transfers between devices  184 us
    all_gather x1, waiting for transfers between devices, on_device(): lax.all_gather(normed_local, 'gx', axis=1, tiled=True)  54.8 us
    psum x1, blocking collectives, on_device(): lax.psum((jnp.sum(state32, axis=1), jnp.sum(state32 * state32, axis=1)),...  34.9 us
    all_to_all x1, blocking collectives, on_device(): lax.all_to_all(attended_rows, 'gx', split_axis=1, concat_axis=0, tiled=True)  15.5 us
    unnamed x13, local copies, waits for them, and re-layouts  12.6 us
    dot_general x1, matrix products, on_device(): jnp.dot(attended, out_weight, preferred_element_type=jnp.float32)  12.2 us
    dot_general x1, matrix products, on_device(): jnp.dot(lax.all_gather(normed_local, 'gx', axis=1, tiled=True), query_wei...  11.3 us
  transfers between devices with their start and end apart: 4, of which 3 were waited for; matrix products, arithmetic and copies ran while one was open for 4% of the time, Pallas kernels for 0%

commit v1 on v0

--- a/solution.py
+++ b/solution.py
@@ -1,10 +1,12 @@
 import jax
 import jax.numpy as jnp
 from jax import lax
+from jax.experimental import pallas as pl
+from jax.experimental.pallas import tpu as pltpu
 from jax.sharding import PartitionSpec as P
 
 
-def on_device(
+def plain_device(
     hidden_state, norm_gain, query_weight, keyval_weight, out_weight, cache_entries, cache_lengths
 ):
     members = lax.axis_size("gx")
@@ -66,6 +68,524 @@
     return (hidden_state.astype(jnp.float32) + summed).astype(jnp.bfloat16)
 
 
+MESH = pl.DeviceIdType.MESH
+PAD = 16
+DEPTH = 4
+
+
+def remote(src, dst, send, recv, peer):
+    return pltpu.make_async_remote_copy(
+        src_ref=src,
+        dst_ref=dst,
+        send_sem=send,
+        recv_sem=recv,
+        device_id={"gx": peer},
+        device_id_type=MESH,
+    )
+
+
+def meet_all(members, me):
+    barrier = pltpu.get_barrier_semaphore()
+    for k in range(1, members):
+        pl.semaphore_signal(
+            barrier, inc=1, device_id={"gx": (me + k) % members}, device_id_type=MESH
+        )
+    pl.semaphore_wait(barrier, members - 1)
+
+
+def place():
+    me = lax.axis_index("gx")
+    return me, me // 4, (me // 2) % 2, me % 2
+
+
+def far_to_near(z):
+    first = 3 * (1 - z // 2)
+    third = 1 + z % 2
+    return [first, 6 - z - first - third, third, z]
+
+
+def slot_of(z, y, c):
+    return z * 4 + y * 2 + c
+
+
+def query_kernel(
+    head_scale,
+    x_ref,
+    note_ref,
+    wq_hbm,
+    kvw_ref,
+    sel_ref,
+    q_out,
+    kv_out,
+    buf,
+    notes,
+    wbuf,
+    acc,
+    stat,
+    q_send,
+    q_got,
+    kv_send,
+    kv_got,
+    w_sem,
+    own_sem,
+    z_sem,
+    y_sem,
+    c_sem,
+    recv_sem,
+    note_sem,
+    kv_sem,
+    q_sem,
+):
+    members = buf.shape[0]
+    rows, width = x_ref.shape
+    total_width = width * members
+    me, z, y, c = place()
+    sibling = slot_of(z, y, 1 - c)
+    across = slot_of(z, 1 - y, c)
+    above = slot_of(jnp.minimum(z + 1, DEPTH - 1), y, c)
+    below = slot_of(jnp.maximum(z - 1, 0), y, c)
+
+    def weights_copy(slot):
+        start = pl.multiple_of(slot * width, 128)
+        return pltpu.make_async_copy(
+            wq_hbm.at[pl.ds(start, width), :], wbuf.at[slot], w_sem.at[slot]
+        )
+
+    own = pltpu.make_async_copy(x_ref, buf.at[me], own_sem)
+    own.start()
+    notes[me] = note_ref[...]
+    order = far_to_near(z)[::-1]
+    own.wait()
+    meet_all(members, me)
+
+    def shard(slot, send, peer):
+        return remote(buf.at[slot], buf.at[slot], send, recv_sem.at[slot], peer)
+
+    def up(zz):
+        return shard(slot_of(zz, y, c), z_sem.at[0, zz], above)
+
+    def down(zz):
+        return shard(slot_of(zz, y, c), z_sem.at[1, zz], below)
+
+    def over(zz):
+        return shard(slot_of(zz, y, c), y_sem.at[zz], across)
+
+    def aside(zz, yy):
+        return shard(slot_of(zz, yy, c), c_sem.at[zz * 2 + yy], sibling)
+
+    def arrived(slot):
+        shard(slot, own_sem, sibling).wait_recv()
+
+    def spread(src_of, dst, sems):
+        for k in range(1, members):
+            peer = (me + k) % members
+            remote(src_of(peer), dst.at[me], sems.at[0, peer], sems.at[1, me], peer).start()
+
+    def collect(src_of, dst, sems):
+        for k in range(1, members):
+            peer = (me + k) % members
+            remote(src_of(peer), dst.at[peer], sems.at[0, peer], sems.at[1, peer], peer).wait()
+
+    spread(lambda peer: note_ref, notes, note_sem)
+    over(z).start()
+
+    @pl.when(z < DEPTH - 1)
+    def _():
+        up(z).start()
+
+    @pl.when(z > 0)
+    def _():
+        down(z).start()
+
+    aside(z, y).start()
+    for slot in range(members):
+        weights_copy(slot).start()
+    collect(lambda peer: note_ref, notes, note_sem)
+
+    mean = jnp.sum(notes[:, 0:2, :], axis=0) / total_width
+    var = jnp.sum(notes[:, 2:4, :], axis=0) / total_width - mean * mean
+    inv = lax.rsqrt(var + 1e-05)
+    stat[0, 0:128, :] = jnp.broadcast_to(mean[0:1, :], (128, 128)).T
+    stat[1, 0:128, :] = jnp.broadcast_to(inv[0:1, :], (128, 128)).T
+    stat[0, 128:rows, :] = jnp.broadcast_to(mean[1:2, :], (128, 128)).T[0 : rows - 128]
+    stat[1, 128:rows, :] = jnp.broadcast_to(inv[1:2, :], (128, 128)).T[0 : rows - 128]
+
+    def normed(slot):
+        tiles = []
+        for t in range(width // 128):
+            part = buf[slot, :, t * 128 : (t + 1) * 128].astype(jnp.float32)
+            gain = notes[slot, 4 + t : 5 + t, :]
+            tiles.append(((part - stat[0]) * stat[1] * gain).astype(jnp.bfloat16))
+        return jnp.concatenate(tiles, axis=1)
+
+    kv = jnp.dot(normed(me), kvw_ref[...], preferred_element_type=jnp.float32)
+    kv = jnp.dot(sel_ref[...], kv.astype(jnp.bfloat16), preferred_element_type=jnp.float32)
+    kv_send[...] = kv.astype(jnp.bfloat16).reshape(kv_send.shape)
+    spread(lambda peer: kv_send.at[peer], kv_got, kv_sem)
+    kv_got[me] = kv_send[me]
+    acc[...] = jnp.zeros_like(acc)
+
+    def work(zz, yy):
+        def one(k, carry):
+            slot = slot_of(zz, yy, (c + k) % 2)
+
+            @pl.when(k == 1)
+            def _():
+                arrived(slot)
+
+            weights_copy(slot).wait()
+            acc[...] += jnp.dot(normed(slot), wbuf[slot], preferred_element_type=jnp.float32)
+            return carry
+
+        lax.fori_loop(0, 2, one, 0)
+
+    work(z, y)
+    for i in range(1, DEPTH):
+
+        @pl.when(z - i >= 0)
+        def _():
+            arrived(slot_of(jnp.maximum(z - i, 0), y, c))
+
+            @pl.when(z < DEPTH - 1)
+            def _():
+                up(jnp.maximum(z - i, 0)).start()
+
+        @pl.when(z + i < DEPTH)
+        def _():
+            arrived(slot_of(jnp.minimum(z + i, DEPTH - 1), y, c))
+
+            @pl.when(z > 0)
+            def _():
+                down(jnp.minimum(z + i, DEPTH - 1)).start()
+
+        over(order[i]).start()
+        aside(order[i], y).start()
+        arrived(slot_of(order[i - 1], 1 - y, c))
+        aside(order[i - 1], 1 - y).start()
+        work(order[i], y)
+        work(order[i - 1], 1 - y)
+    arrived(slot_of(order[DEPTH - 1], 1 - y, c))
+    aside(order[DEPTH - 1], 1 - y).start()
+    work(order[DEPTH - 1], 1 - y)
+
+    query = (acc[...] * head_scale).astype(jnp.bfloat16)
+    query = jnp.dot(sel_ref[...], query, preferred_element_type=jnp.float32)
+    q_send[...] = query.astype(jnp.bfloat16).reshape(q_send.shape)
+    spread(lambda peer: q_send.at[peer], q_got, q_sem)
+    q_got[me] = q_send[me]
+    collect(lambda peer: kv_send.at[peer], kv_got, kv_sem)
+    kv_out[...] = jnp.sum(kv_got[...].astype(jnp.float32), axis=0).astype(jnp.bfloat16)
+    for zz in range(DEPTH):
+        over(zz).wait_send()
+        aside(zz, 0).wait_send()
+        aside(zz, 1).wait_send()
+
+        @pl.when((z < DEPTH - 1) & (zz <= z))
+        def _():
+            up(zz).wait_send()
+
+        @pl.when((z > 0) & (zz >= z))
+        def _():
+            down(zz).wait_send()
+
+    collect(lambda peer: q_send.at[peer], q_got, q_sem)
+    q_out[...] = q_got[...]
+
+
+def query_call(x, note, wq, kvw, sel, members, head_scale):
+    rows, width = x.shape
+    cols = wq.shape[1]
+    vmem = pl.BlockSpec(memory_space=pltpu.VMEM)
+    swap = (members, PAD, cols)
+    kv_cols = kvw.shape[1]
+    dma = pltpu.SemaphoreType.DMA
+    return pl.pallas_call(
+        lambda *refs: query_kernel(head_scale, *refs),
+        out_shape=(
+            jax.ShapeDtypeStruct(swap, jnp.bfloat16),
+            jax.ShapeDtypeStruct((PAD, kv_cols), jnp.bfloat16),
+        ),
+        in_specs=[vmem, vmem, pl.BlockSpec(memory_space=pl.ANY), vmem, vmem],
+        out_specs=(vmem, vmem),
+        scratch_shapes=[
+            pltpu.VMEM((members, rows, width), jnp.bfloat16),
+            pltpu.VMEM((members,) + note.shape, jnp.float32),
+            pltpu.VMEM((members, width, cols), jnp.bfloat16),
+            pltpu.VMEM((rows, cols), jnp.float32),
+            pltpu.VMEM((2, rows, 128), jnp.float32),
+            pltpu.VMEM(swap, jnp.bfloat16),
+            pltpu.VMEM(swap, jnp.bfloat16),
+            pltpu.VMEM((members, PAD, kv_cols), jnp.bfloat16),
+            pltpu.VMEM((members, PAD, kv_cols), jnp.bfloat16),
+            dma((members,)),
+            dma,
+            dma((2, DEPTH)),
+            dma((DEPTH,)),
+            dma((2 * DEPTH,)),
+            dma((members,)),
+            dma((2, members)),
+            dma((2, members)),
+            dma((2, members)),
+        ],
+        compiler_params=pltpu.CompilerParams(
+            collective_id=0, has_side_effects=True, vmem_limit_bytes=48 * 1024 * 1024
+        ),
+    )(x, note, wq, kvw, sel)
+
+
+def output_kernel(
+    att_ref,
+    pick_ref,
+    wo_hbm,
+    out_ref,
+    att_got,
+    att,
+    wbuf,
+    mine,
+    c_send,
+    c_got,
+    y_send,
+    y_got,
+    z_send,
+    z_got,
+    w_sem,
+    att_sem,
+    c_sem,
+    y_sem,
+    z_sem,
+):
+    members = att_ref.shape[0]
+    rows, width = out_ref.shape
+    me, z, y, c = place()
+    sibling = slot_of(z, y, 1 - c)
+    across = slot_of(z, 1 - y, c)
+    above = slot_of(jnp.minimum(z + 1, DEPTH - 1), y, c)
+    below = slot_of(jnp.maximum(z - 1, 0), y, c)
+    order = far_to_near(z)
+
+    def weights_copy(slot):
+        start = pl.multiple_of(slot * width, 128)
+        return pltpu.make_async_copy(
+            wo_hbm.at[:, pl.ds(start, width)], wbuf.at[slot], w_sem.at[slot]
+        )
+
+    for zz in order:
+        for yy in (1 - y, y):
+            for cc in (1 - c, c):
+                weights_copy(slot_of(zz, yy, cc)).start()
+    meet_all(members, me)
+
+    def swap(k):
+        peer = (me + k) % members
+        return peer, att_ref.at[peer], att_sem.at[0, peer]
+
+    for k in range(1, members):
+        peer, src, sem = swap(k)
+        remote(src, att_got.at[me], sem, att_sem.at[1, me], peer).start()
+    att_got[me] = att_ref[me]
+    for k in range(1, members):
+        peer, src, sem = swap(k)
+        remote(src, att_got.at[peer], sem, att_sem.at[1, peer], peer).wait()
+    gathered = att_got[...].reshape(members * PAD, att.shape[1])
+    att[...] = jnp.dot(
+        pick_ref[...], gathered, preferred_element_type=jnp.float32
+    ).astype(jnp.bfloat16)
+
+    tile = width // 3 if width % 384 == 0 else width
+
+    def product(slot, store):
+        weights_copy(slot).wait()
+
+        def one(t, carry):
+            cols = pl.ds(pl.multiple_of(t * tile, 128), tile)
+            store(
+                cols, jnp.dot(att[...], wbuf[slot, :, cols], preferred_element_type=jnp.float32)
+            )
+            return carry
+
+        lax.fori_loop(0, width // tile, one, 0)
+
+    def aside(p):
+        return remote(c_send.at[p], c_got.at[p], c_sem.at[0, p], c_sem.at[1, p], sibling)
+
+    def over(i):
+        return remote(y_send.at[i], y_got.at[i], y_sem.at[0, i], y_sem.at[1, i], across)
+
+    def up(zz):
+        return remote(
+            z_send.at[zz], z_got.at[0, zz], z_sem.at[0, zz], z_sem.at[1, zz], above
+        )
+
+    def down(zz):
+        return remote(
+            z_send.at[zz], z_got.at[1, zz], z_sem.at[0, zz], z_sem.at[2, zz], below
+        )
+
+    for i in range(DEPTH):
+        for j, yy in enumerate((1 - y, y)):
+            p = 2 * i + j
+
+            def to_sibling(cols, value):
+                c_send[p, :, cols] = value.astype(jnp.bfloat16)
+
+            product(slot_of(order[i], yy, 1 - c), to_sibling)
+            aside(p).start()
+        for j, yy in enumerate((1 - y, y)):
+            p = 2 * i + j
+
+            def keep(cols, value):
+                mine[i, :, cols] = value
+
+            product(slot_of(order[i], yy, c), keep)
+            aside(p).wait_recv()
+            if j == 0:
+                y_send[i] = (mine[i] + c_got[p].astype(jnp.float32)).astype(jnp.bfloat16)
+                over(i).start()
+            else:
+                mine[i] += c_got[p].astype(jnp.float32)
+
+    for i in range(DEPTH - 1):
+        zz = order[i]
+        over(i).wait_recv()
+        mine[i] += y_got[i].astype(jnp.float32)
+
+        @pl.when(zz > z)
+        def _():
+            @pl.when(z > 0)
+            def _():
+                up(zz).wait_recv()
+                mine[i] += z_got[0, zz].astype(jnp.float32)
+
+            z_send[zz] = mine[i].astype(jnp.bfloat16)
+            up(zz).start()
+
+        @pl.when(zz < z)
+        def _():
+            @pl.when(z < DEPTH - 1)
+            def _():
+                down(zz).wait_recv()
+                mine[i] += z_got[1, zz].astype(jnp.float32)
+
+            z_send[zz] = mine[i].astype(jnp.bfloat16)
+            down(zz).start()
+
+    last = DEPTH - 1
+    over(last).wait_recv()
+    mine[last] += y_got[last].astype(jnp.float32)
+
+    @pl.when(z > 0)
+    def _():
+        up(z).wait_recv()
+        mine[last] += z_got[0, z].astype(jnp.float32)
+
+    @pl.when(z < DEPTH - 1)
+    def _():
+        down(z).wait_recv()
+        mine[last] += z_got[1, z].astype(jnp.float32)
+
+    out_ref[...] = mine[last]
+    for i in range(DEPTH):
+        over(i).wait_send()
+        aside(2 * i).wait_send()
+        aside(2 * i + 1).wait_send()
+    for i in range(DEPTH - 1):
+        up(order[i]).wait_send()
+
+
+def output_call(att, pick, wo, members, width):
+    rows = pick.shape[0]
+    depth = wo.shape[0]
+    vmem = pl.BlockSpec(memory_space=pltpu.VMEM)
+    dma = pltpu.SemaphoreType.DMA
+    block = (rows, width)
+    return pl.pallas_call(
+        output_kernel,
+        out_shape=jax.ShapeDtypeStruct(block, jnp.float32),
+        in_specs=[vmem, vmem, pl.BlockSpec(memory_space=pl.ANY)],
+        out_specs=vmem,
+        scratch_shapes=[
+            pltpu.VMEM(att.shape, jnp.bfloat16),
+            pltpu.VMEM((rows, depth), jnp.bfloat16),
+            pltpu.VMEM((members, depth, width), jnp.bfloat16),
+            pltpu.VMEM((DEPTH,) + block, jnp.float32),
+            pltpu.VMEM((2 * DEPTH,) + block, jnp.bfloat16),
+            pltpu.VMEM((2 * DEPTH,) + block, jnp.bfloat16),
+            pltpu.VMEM((DEPTH,) + block, jnp.bfloat16),
+            pltpu.VMEM((DEPTH,) + block, jnp.bfloat16),
+            pltpu.VMEM((DEPTH,) + block, jnp.bfloat16),
+            pltpu.VMEM((2, DEPTH) + block, jnp.bfloat16),
+            dma((members,)),
+            dma((2, members)),
+            dma((2, 2 * DEPTH)),
+            dma((2, DEPTH)),
+            dma((3, DEPTH)),
+        ],
+        compiler_params=pltpu.CompilerParams(
+            collective_id=1, has_side_effects=True, vmem_limit_bytes=56 * 1024 * 1024
+        ),
+    )(att, pick, wo)
+
+
+def attention(query3, new_entry, cache_entries, cache_lengths):
+    head_size = query3.shape[2]
+    keys = cache_entries[:, :, :head_size]
+    values = cache_entries[:, :, head_size:]
+    scores = jnp.einsum("rhd,rld->rhl", query3, keys, preferred_element_type=jnp.float32)
+    fresh = jnp.einsum(
+        "rhd,rd->rh", query3, new_entry[:, :head_size], preferred_element_type=jnp.float32
+    )
+    valid = jnp.arange(keys.shape[1])[None, :] < cache_lengths[:, None]
+    scores = jnp.where(valid[:, None, :], scores, -1e30)
+    peak = jnp.maximum(jnp.max(scores, axis=-1), fresh)
+    weights = jnp.exp(scores - peak[..., None]) * valid[:, None, :].astype(jnp.float32)
+    fresh_w = jnp.exp(fresh - peak)
+    total = jnp.sum(weights, axis=-1) + fresh_w
+    probs = (weights / total[..., None]).astype(jnp.bfloat16)
+    fresh_p = (fresh_w / total).astype(jnp.bfloat16)
+    mixed = jnp.einsum("rhl,rld->rhd", probs, values, preferred_element_type=jnp.float32)
+    mixed = mixed + fresh_p.astype(jnp.float32)[..., None] * new_entry[:, None, head_size:].astype(
+        jnp.float32
+    )
+    return mixed.astype(jnp.bfloat16)
+
+
+def fast_device(
+    hidden_state, norm_gain, query_weight, keyval_weight, out_weight, cache_entries, cache_lengths
+):
+    members = lax.axis_size("gx")
+    rows_all, width = hidden_state.shape
+    rows = rows_all // members
+    head_size = keyval_weight.shape[1] // 2
+    cols = query_weight.shape[1]
+    state32 = hidden_state.astype(jnp.float32)
+    sums = jnp.stack([jnp.sum(state32, axis=1), jnp.sum(state32 * state32, axis=1)])
+    sums = jnp.pad(sums, ((0, 0), (0, 256 - rows_all))).reshape(4, 128)
+    note = jnp.concatenate([sums, norm_gain.reshape(-1, 128)], axis=0)
+    note = jnp.pad(note, ((0, -note.shape[0] % 8), (0, 0)))
+    padded = jnp.arange(members * PAD)
+    source = jnp.where(padded % PAD < rows, padded // PAD * rows + padded % PAD, -1)
+    select = (source[:, None] == jnp.arange(rows_all)[None, :]).astype(jnp.bfloat16)
+    pick = (source[None, :] == jnp.arange(rows_all)[:, None]).astype(jnp.bfloat16)
+    q_rows, kv_rows = query_call(
+        hidden_state, note, query_weight, keyval_weight, select, members, head_size ** (-0.5)
+    )
+    query3 = q_rows[:, :rows].transpose(1, 0, 2).reshape(rows, -1, head_size)
+    mixed = attention(query3, kv_rows[:rows], cache_entries, cache_lengths)
+    att = mixed.reshape(rows, members, cols).transpose(1, 0, 2)
+    att = jnp.pad(att, ((0, 0), (0, PAD - rows), (0, 0)))
+    summed = output_call(att, pick, out_weight, members, width)
+    return (hidden_state.astype(jnp.float32) + summed).astype(jnp.bfloat16)
+
+
+def on_device(hidden_state, *others):
+    members = lax.axis_size("gx")
+    rows_all, width = hidden_state.shape
+    fits = width % 128 == 0 and 128 < rows_all <= 256 and rows_all % 16 == 0
+    if members == 4 * DEPTH and fits and rows_all // members <= PAD:
+        return fast_device(hidden_state, *others)
+    return plain_device(hidden_state, *others)
+
+
 def solution(mesh):
     in_specs = (
         P("groups", "gx"),

time: 357 us -> 127 us (0.36)
  waiting for transfers between devices: 239 us -> 0 us
  Pallas kernels: 0 us -> 112 us
  blocking collectives: 50.4 us -> 0 us
  matrix products: 30.8 us -> 5.2 us
  between operations: 13.9 us -> 0.12 us
  local copies, waits for them, and re-layouts: 13.7 us -> 3.33 us
  starting transfers between devices: 3.62 us -> 0 us
    unnamed x5 -> x0, waiting for transfers between devices: 184 us -> none
    pallas_call x0 -> x2, Pallas kernels: none -> 112 us  [the longest x1 57.6 us: query_call(): pl.pallas_call(lambda *refs: query_kernel(head_scale, *refs), out_shape=(...]
    all_gather x1 -> x0, waiting for transfers between devices: 54.8 us -> none  [on_device(): lax.all_gather(normed_local, 'gx', axis=1, tiled=True)]
    psum x1 -> x0, blocking collectives: 34.9 us -> none  [on_device(): lax.psum((jnp.sum(state32, axis=1), jnp.sum(state32 * state32, axis=1)),...]
    dot_general x6 -> x3, matrix products: 30.8 us -> 5.2 us  [the longest x1 2.7 us: attention(): jnp.einsum('rhd,rld->rhl', query3, keys, preferred_element_type=jnp.float32)]
    all_to_all x1 -> x0, blocking collectives: 15.5 us -> none  [on_device(): lax.all_to_all(attended_rows, 'gx', split_axis=1, concat_axis=0, tiled=True)]
    unnamed x13 -> x6, local copies, waits for them, and re-layouts: 12.6 us -> 2.26 us
  transfers between devices with their start and end apart: 4 -> 0, of which waited for: 3 -> 0; matrix products, arithmetic and copies ran while one was open for 4% -> 0% of each run, Pallas kernels for 0% -> 0%
where the time goes in v1:
time: 127 us
  Pallas kernels  112 us (88%)
  other arithmetic  5.57 us (4%)
  matrix products  5.2 us (4%)
  local copies, waits for them, and re-layouts  3.33 us (3%)
    pallas_call x1, Pallas kernels, query_call(): pl.pallas_call(lambda *refs: query_kernel(head_scale, *refs), out_shape=(...  57.6 us
    pallas_call x1, Pallas kernels, output_call(): pl.pallas_call(output_kernel, out_shape=jax.ShapeDtypeStruct(block, jnp.f...  54.8 us
    dot_general x1, matrix products, attention(): jnp.einsum('rhd,rld->rhl', query3, keys, preferred_element_type=jnp.float32)  2.7 us

profile of v1, /device:TPU:0, one launch (start us, length us, event | category | flops | bytes accessed | tf_op | source)
XLA Modules:
  0.0 126.7 jit_solution(7958846287938087286)
XLA Ops:
  0.0 1.2 convert_reduce_fusion
  1.2 0.7 select_maximum_fusion.refs_1_
  1.9 0.7 fusion.30
  2.7 0.6 fusion.20.pick_ref
  3.3 0.1 fusion.19.refs_4_
  3.4 0.0 copy-start
  3.4 1.0 copy-done
  4.4 0.0 copy-start.2
  4.4 1.3 %copy-done.2 = bf16[1152,512]{1,0:T(8,128)(2,1)S(1)} copy-done((bf16[1152,512]{1,0:T(8,128)(2,1)S(1)}, bf16[1152,512]{1,0:T(8,128)(2,1)}, u32[]{:S(2)}) %copy-start.2) | copy-done | bytes 1179672
  5.7 57.6 %shard_map.73 = (bf16[16,16,512]{2,1,0:T(8,128)(2,1)S(1)}, bf16[16,512]{1,0:T(8,128)(2,1)S(1)}) custom-call(bf16[160,1152]{1,0:T(8,128)(2,1)S(1)} %copy-done, f32[16,128]{1,0:T(8,128)S(1)} %select_maximum_fusion.refs_1_, bf16[18432,512]{1,0:T(8,128)(2,1)} %refs_2_.1, bf16[1152,512]{1,0:T(8,128)(2,1)S(1)} %copy-done.2, bf16[256,160]{1,0:T(8,128)(2,1)S(1)} %fusion.19.refs_4_), custom_call_target="tpu_custom_call" | custom-call | tf_op jit(solution)/shard_map/pallas_call | solution.py:302
  63.3 0.1 copy.8
  63.4 0.1 reshape.99
  63.5 0.1 fusion.21
  63.7 2.7 %fusion.31 = (f32[10,32]{1,0:T(8,128)S(1)}, f32[10,32,512]{2,1,0:T(8,128)S(1)}) fusion(bf16[10,32,256]{2,1,0:T(8,128)(2,1)S(1)} %reshape.99, bf16[10,512,512]{2,1,0:T(8,128)(2,1)} %param.12, pred[10,512]{1,0:T(8,128)(4,1)S(1)} %get-tuple-element.16), kind=kOutput, calls=%fused_computation.49 | convolution fusion | flops 84213440 | bytes 3447040 | tf_op jit(solution)/shard_map/rhd,rld->rhl/dot_general | solution.py:533
  66.4 0.3 fusion.15
  66.7 2.4 %fusion.10 = bf16[10,32,256]{2,1,0:T(8,128)(2,1)S(1)} fusion(bf16[10,512,512]{2,1,0:T(8,128)(2,1)} %param.12, f32[10,32,512]{2,1,0:T(8,128)S(1)} %get-tuple-element.18, f32[10,32]{1,0:T(8,128)S(1)} %get-tuple-element.12, f32[10,512]{1,0:T(8,128)S(1)} %get-tuple-element.15, f32[10,32]{1,0:T(8,128)S(1)} %bitcast_maximum_fusion, ...), kind=kOutput, calls=%fused_computation.6 | convolution fusion | flops 84787200 | bytes 3475200 | tf_op jit(solution)/shard_map/rhl,rld->rhd/dot_general | solution.py:545
  69.0 0.1 reshape.100
  69.1 0.1 copy.31
  69.2 0.7 pad.14.att_ref
  69.9 0.0 copy-start.1
  69.9 54.8 %shard_map.74 = f32[160,1152]{1,0:T(8,128)} custom-call(bf16[16,16,512]{2,1,0:T(8,128)(2,1)} %pad.14.att_ref, bf16[160,256]{1,0:T(8,128)(2,1)} %fusion.20.pick_ref, bf16[512,18432]{1,0:T(8,128)(2,1)} %wo_hbm.1), custom_call_target="tpu_custom_call" | custom-call | tf_op jit(solution)/shard_map/pallas_call | solution.py:501
  124.8 0.0 copy-done.1
  124.8 1.9 %fusion.14 = bf16[160,1152]{1,0:T(8,128)(2,1)} fusion(f32[160,1152]{1,0:T(8,128)} %shard_map.74, bf16[160,1152]{1,0:T(8,128)(2,1)S(1)} %copy-done.1), kind=kLoop, calls=%fused_computation.11 | loop fusion | flops 552960 | bytes 1474560 | tf_op jit(solution)/shard_map/convert_element_type | solution.py:577
  (7 shorter events, 0.1 us)
Async XLA Ops:
  3.4 1.0 copy-start
  4.4 1.3 %copy-start.2 = (bf16[1152,512]{1,0:T(8,128)(2,1)S(1)}, bf16[1152,512]{1,0:T(8,128)(2,1)}, u32[]{:S(2)}) copy-start(bf16[1152,512]{1,0:T(8,128)(2,1)} %refs_3_.1) | copy-start | bytes 3538948
  69.9 54.8 %copy-start.1 = (bf16[160,1152]{1,0:T(8,128)(2,1)S(1)}, bf16[160,1152]{1,0:T(8,128)(2,1)}, u32[]{:S(2)}) copy-start(bf16[160,1152]{1,0:T(8,128)(2,1)} %refs_0_.1) | copy-start | bytes 1105924

commit v2 on v1

--- a/solution.py
+++ b/solution.py
@@ -71,6 +71,7 @@
 MESH = pl.DeviceIdType.MESH
 PAD = 16
 DEPTH = 4
+FIRST = 32
 
 
 def remote(src, dst, send, recv, peer):
@@ -104,22 +105,36 @@
     return [first, 6 - z - first - third, third, z]
 
 
+def pieces(rows):
+    half = (rows - FIRST) // 2
+    return [pl.ds(0, FIRST), pl.ds(FIRST, half), pl.ds(FIRST + half, half)]
+
+
+def spread_rows(members, rows, local, flip):
+    shape = (rows, members * PAD) if flip else (members * PAD, rows)
+    p = lax.broadcasted_iota(jnp.int32, shape, 1 if flip else 0)
+    r = lax.broadcasted_iota(jnp.int32, shape, 0 if flip else 1)
+    inner = p & (PAD - 1)
+    hit = (inner < local) & ((p >> 4) * local + inner == r)
+    return jnp.where(hit, 1.0, 0.0).astype(jnp.bfloat16)
+
+
 def slot_of(z, y, c):
     return z * 4 + y * 2 + c
 
 
 def query_kernel(
     head_scale,
-    x_ref,
+    x_hbm,
     note_ref,
     wq_hbm,
-    kvw_ref,
-    sel_ref,
+    kvw_hbm,
     q_out,
     kv_out,
     buf,
     notes,
     wbuf,
+    kvw,
     acc,
     stat,
     q_send,
@@ -137,7 +152,8 @@
     q_sem,
 ):
     members = buf.shape[0]
-    rows, width = x_ref.shape
+    rows, width = x_hbm.shape
+    parts = pieces(rows)
     total_width = width * members
     me, z, y, c = place()
     sibling = slot_of(z, y, 1 - c)
@@ -151,30 +167,66 @@
             wq_hbm.at[pl.ds(start, width), :], wbuf.at[slot], w_sem.at[slot]
         )
 
-    own = pltpu.make_async_copy(x_ref, buf.at[me], own_sem)
+    own = pltpu.make_async_copy(x_hbm, buf.at[me], own_sem.at[0])
     own.start()
+    kvw_copy = pltpu.make_async_copy(kvw_hbm, kvw, own_sem.at[1])
+    kvw_copy.start()
     notes[me] = note_ref[...]
     order = far_to_near(z)[::-1]
     own.wait()
     meet_all(members, me)
 
-    def shard(slot, send, peer):
-        return remote(buf.at[slot], buf.at[slot], send, recv_sem.at[slot], peer)
-
-    def up(zz):
-        return shard(slot_of(zz, y, c), z_sem.at[0, zz], above)
-
-    def down(zz):
-        return shard(slot_of(zz, y, c), z_sem.at[1, zz], below)
-
-    def over(zz):
-        return shard(slot_of(zz, y, c), y_sem.at[zz], across)
+    def shard(slot, piece, send, peer):
+        rows_of = pl.ds(0, rows) if piece == 3 else parts[piece]
+        block = buf.at[slot, rows_of, :]
+        return remote(block, block, send, recv_sem.at[slot, piece], peer)
+
+    def up(zz, k):
+        yy = 1 - y if k == 3 else y
+        return shard(slot_of(zz, yy, c), k % 3, z_sem.at[0, zz, k], above)
+
+    def down(zz, k):
+        yy = 1 - y if k == 3 else y
+        return shard(slot_of(zz, yy, c), k % 3, z_sem.at[1, zz, k], below)
+
+    def over(zz, k):
+        return shard(slot_of(zz, y, c), k, y_sem.at[zz, k], across)
 
     def aside(zz, yy):
-        return shard(slot_of(zz, yy, c), c_sem.at[zz * 2 + yy], sibling)
-
-    def arrived(slot):
-        shard(slot, own_sem, sibling).wait_recv()
+        return shard(slot_of(zz, yy, c), 3, c_sem.at[zz * 2 + yy], sibling)
+
+    def arrived(slot, piece):
+        shard(slot, piece, own_sem.at[0], sibling).wait_recv()
+
+    def both_ways(k):
+        @pl.when(z < DEPTH - 1)
+        def _():
+            up(z, k).start()
+
+        @pl.when(z > 0)
+        def _():
+            down(z, k).start()
+
+    def relay(i, k):
+        yy = 1 - y if k == 3 else y
+
+        @pl.when(z - i >= 0)
+        def _():
+            low = jnp.maximum(z - i, 0)
+            arrived(slot_of(low, yy, c), k % 3)
+
+            @pl.when(z < DEPTH - 1)
+            def _():
+                up(low, k).start()
+
+        @pl.when(z + i < DEPTH)
+        def _():
+            high = jnp.minimum(z + i, DEPTH - 1)
+            arrived(slot_of(high, yy, c), k % 3)
+
+            @pl.when(z > 0)
+            def _():
+                down(high, k).start()
 
     def spread(src_of, dst, sems):
         for k in range(1, members):
@@ -187,16 +239,12 @@
             remote(src_of(peer), dst.at[peer], sems.at[0, peer], sems.at[1, peer], peer).wait()
 
     spread(lambda peer: note_ref, notes, note_sem)
-    over(z).start()
-
-    @pl.when(z < DEPTH - 1)
-    def _():
-        up(z).start()
-
-    @pl.when(z > 0)
-    def _():
-        down(z).start()
-
+    over(z, 0).start()
+    both_ways(1)
+    over(z, 1).start()
+    both_ways(2)
+    over(z, 2).start()
+    both_ways(0)
     aside(z, y).start()
     for slot in range(members):
         weights_copy(slot).start()
@@ -218,8 +266,12 @@
             tiles.append(((part - stat[0]) * stat[1] * gain).astype(jnp.bfloat16))
         return jnp.concatenate(tiles, axis=1)
 
-    kv = jnp.dot(normed(me), kvw_ref[...], preferred_element_type=jnp.float32)
-    kv = jnp.dot(sel_ref[...], kv.astype(jnp.bfloat16), preferred_element_type=jnp.float32)
+    arrived(slot_of(z, 1 - y, c), 0)
+    both_ways(3)
+    kvw_copy.wait()
+    select = spread_rows(members, rows, rows // members, False)
+    kv = jnp.dot(normed(me), kvw[...], preferred_element_type=jnp.float32)
+    kv = jnp.dot(select, kv.astype(jnp.bfloat16), preferred_element_type=jnp.float32)
     kv_send[...] = kv.astype(jnp.bfloat16).reshape(kv_send.shape)
     spread(lambda peer: kv_send.at[peer], kv_got, kv_sem)
     kv_got[me] = kv_send[me]
@@ -231,7 +283,7 @@
 
             @pl.when(k == 1)
             def _():
-                arrived(slot)
+                arrived(slot, 3)
 
             weights_copy(slot).wait()
             acc[...] += jnp.dot(normed(slot), wbuf[slot], preferred_element_type=jnp.float32)
@@ -239,63 +291,64 @@
 
         lax.fori_loop(0, 2, one, 0)
 
-    work(z, y)
+    def finish_across(i):
+        slot = slot_of(order[i], 1 - y, c)
+        arrived(slot, 1)
+        arrived(slot, 2)
+        aside(order[i], 1 - y).start()
+
     for i in range(1, DEPTH):
-
-        @pl.when(z - i >= 0)
-        def _():
-            arrived(slot_of(jnp.maximum(z - i, 0), y, c))
-
-            @pl.when(z < DEPTH - 1)
-            def _():
-                up(jnp.maximum(z - i, 0)).start()
-
-        @pl.when(z + i < DEPTH)
-        def _():
-            arrived(slot_of(jnp.minimum(z + i, DEPTH - 1), y, c))
-
-            @pl.when(z > 0)
-            def _():
-                down(jnp.minimum(z + i, DEPTH - 1)).start()
-
-        over(order[i]).start()
+        relay(i, 1)
+        over(order[i], 1).start()
+        work(order[i - 1], y)
+        relay(i, 2)
+        over(order[i], 2).start()
+        finish_across(i - 1)
+        relay(i, 0)
         aside(order[i], y).start()
-        arrived(slot_of(order[i - 1], 1 - y, c))
-        aside(order[i - 1], 1 - y).start()
-        work(order[i], y)
+        relay(i, 3)
         work(order[i - 1], 1 - y)
-    arrived(slot_of(order[DEPTH - 1], 1 - y, c))
-    aside(order[DEPTH - 1], 1 - y).start()
+    work(order[DEPTH - 1], y)
+    finish_across(DEPTH - 1)
     work(order[DEPTH - 1], 1 - y)
 
     query = (acc[...] * head_scale).astype(jnp.bfloat16)
-    query = jnp.dot(sel_ref[...], query, preferred_element_type=jnp.float32)
+    query = jnp.dot(select, query, preferred_element_type=jnp.float32)
     q_send[...] = query.astype(jnp.bfloat16).reshape(q_send.shape)
     spread(lambda peer: q_send.at[peer], q_got, q_sem)
     q_got[me] = q_send[me]
     collect(lambda peer: kv_send.at[peer], kv_got, kv_sem)
     kv_out[...] = jnp.sum(kv_got[...].astype(jnp.float32), axis=0).astype(jnp.bfloat16)
     for zz in range(DEPTH):
-        over(zz).wait_send()
+        for piece in range(3):
+            over_sent = (piece > 0) | (zz == z)
+
+            @pl.when(over_sent)
+            def _():
+                over(zz, piece).wait_send()
+
         aside(zz, 0).wait_send()
         aside(zz, 1).wait_send()
 
         @pl.when((z < DEPTH - 1) & (zz <= z))
         def _():
-            up(zz).wait_send()
+            for piece in range(4):
+                up(zz, piece).wait_send()
 
         @pl.when((z > 0) & (zz >= z))
         def _():
-            down(zz).wait_send()
+            for piece in range(4):
+                down(zz, piece).wait_send()
 
     collect(lambda peer: q_send.at[peer], q_got, q_sem)
     q_out[...] = q_got[...]
 
 
-def query_call(x, note, wq, kvw, sel, members, head_scale):
+def query_call(x, note, wq, kvw, members, head_scale):
     rows, width = x.shape
     cols = wq.shape[1]
     vmem = pl.BlockSpec(memory_space=pltpu.VMEM)
+    hbm = pl.BlockSpec(memory_space=pl.ANY)
     swap = (members, PAD, cols)
     kv_cols = kvw.shape[1]
     dma = pltpu.SemaphoreType.DMA
@@ -305,12 +358,13 @@
             jax.ShapeDtypeStruct(swap, jnp.bfloat16),
             jax.ShapeDtypeStruct((PAD, kv_cols), jnp.bfloat16),
         ),
-        in_specs=[vmem, vmem, pl.BlockSpec(memory_space=pl.ANY), vmem, vmem],
+        in_specs=[hbm, vmem, hbm, hbm],
         out_specs=(vmem, vmem),
         scratch_shapes=[
             pltpu.VMEM((members, rows, width), jnp.bfloat16),
             pltpu.VMEM((members,) + note.shape, jnp.float32),
             pltpu.VMEM((members, width, cols), jnp.bfloat16),
+            pltpu.VMEM(kvw.shape, jnp.bfloat16),
             pltpu.VMEM((rows, cols), jnp.float32),
             pltpu.VMEM((2, rows, 128), jnp.float32),
             pltpu.VMEM(swap, jnp.bfloat16),
@@ -318,11 +372,11 @@
             pltpu.VMEM((members, PAD, kv_cols), jnp.bfloat16),
             pltpu.VMEM((members, PAD, kv_cols), jnp.bfloat16),
             dma((members,)),
-            dma,
-            dma((2, DEPTH)),
-            dma((DEPTH,)),
+            dma((2,)),
+            dma((2, DEPTH, 4)),
+            dma((DEPTH, 3)),
             dma((2 * DEPTH,)),
-            dma((members,)),
+            dma((members, 4)),
             dma((2, members)),
             dma((2, members)),
             dma((2, members)),
@@ -330,12 +384,12 @@
         compiler_params=pltpu.CompilerParams(
             collective_id=0, has_side_effects=True, vmem_limit_bytes=48 * 1024 * 1024
         ),
-    )(x, note, wq, kvw, sel)
+    )(x, note, wq, kvw)
 
 
 def output_kernel(
     att_ref,
-    pick_ref,
+    x_hbm,
     wo_hbm,
     out_ref,
     att_got,
@@ -348,7 +402,9 @@
     y_got,
     z_send,
     z_got,
+    x,
     w_sem,
+    x_sem,
     att_sem,
     c_sem,
     y_sem,
@@ -362,6 +418,9 @@
     above = slot_of(jnp.minimum(z + 1, DEPTH - 1), y, c)
     below = slot_of(jnp.maximum(z - 1, 0), y, c)
     order = far_to_near(z)
+    parts = pieces(rows)
+    lanes = parts + [pl.ds(rows, FIRST)]
+    x_copy = pltpu.make_async_copy(x_hbm, x, x_sem)
 
     def weights_copy(slot):
         start = pl.multiple_of(slot * width, 128)
@@ -373,6 +432,7 @@
         for yy in (1 - y, y):
             for cc in (1 - c, c):
                 weights_copy(slot_of(zz, yy, cc)).start()
+    x_copy.start()
     meet_all(members, me)
 
     def swap(k):
@@ -388,7 +448,8 @@
         remote(src, att_got.at[peer], sem, att_sem.at[1, peer], peer).wait()
     gathered = att_got[...].reshape(members * PAD, att.shape[1])
     att[...] = jnp.dot(
-        pick_ref[...], gathered, preferred_element_type=jnp.float32
+        spread_rows(members, rows, rows // members, True),
+        gathered, preferred_element_type=jnp.float32
     ).astype(jnp.bfloat16)
 
     tile = width // 3 if width % 384 == 0 else width
@@ -408,20 +469,37 @@
     def aside(p):
         return remote(c_send.at[p], c_got.at[p], c_sem.at[0, p], c_sem.at[1, p], sibling)
 
-    def over(i):
-        return remote(y_send.at[i], y_got.at[i], y_sem.at[0, i], y_sem.at[1, i], across)
-
-    def up(zz):
+    def over(i, k):
         return remote(
-            z_send.at[zz], z_got.at[0, zz], z_sem.at[0, zz], z_sem.at[1, zz], above
+            y_send.at[i, parts[k], :],
+            y_got.at[i, parts[k], :],
+            y_sem.at[0, i, k],
+            y_sem.at[1, i, k],
+            across,
         )
 
-    def down(zz):
+    def up(zz, k):
         return remote(
-            z_send.at[zz], z_got.at[1, zz], z_sem.at[0, zz], z_sem.at[2, zz], below
+            z_send.at[zz, lanes[k], :],
+            z_got.at[0, zz, lanes[k], :],
+            z_sem.at[0, zz, k],
+            z_sem.at[1, zz, k],
+            above,
         )
 
-    for i in range(DEPTH):
+    def down(zz, k):
+        return remote(
+            z_send.at[zz, lanes[k], :],
+            z_got.at[1, zz, lanes[k], :],
+            z_sem.at[0, zz, k],
+            z_sem.at[2, zz, k],
+            below,
+        )
+
+    def add(p, k, ref, *place):
+        mine[p, parts[k % 3], :] += ref[(*place, lanes[k], slice(None))].astype(jnp.float32)
+
+    def blocks(i):
         for j, yy in enumerate((1 - y, y)):
             p = 2 * i + j
 
@@ -434,96 +512,135 @@
             p = 2 * i + j
 
             def keep(cols, value):
-                mine[i, :, cols] = value
+                mine[p, :, cols] = value
 
             product(slot_of(order[i], yy, c), keep)
             aside(p).wait_recv()
+            mine[p] += c_got[p].astype(jnp.float32)
             if j == 0:
-                y_send[i] = (mine[i] + c_got[p].astype(jnp.float32)).astype(jnp.bfloat16)
-                over(i).start()
-            else:
-                mine[i] += c_got[p].astype(jnp.float32)
-
-    for i in range(DEPTH - 1):
+                for k in (1, 2):
+                    y_send[i, parts[k], :] = mine[p, parts[k], :].astype(jnp.bfloat16)
+                    over(i, k).start()
+
+    def pass_on(i, k):
         zz = order[i]
-        over(i).wait_recv()
-        mine[i] += y_got[i].astype(jnp.float32)
+        p = 2 * i + (0 if k == 3 else 1)
+
+        def send(step):
+            z_send[zz, lanes[k], :] = mine[p, parts[k % 3], :].astype(jnp.bfloat16)
+            step(zz, k).start()
 
         @pl.when(zz > z)
         def _():
             @pl.when(z > 0)
             def _():
-                up(zz).wait_recv()
-                mine[i] += z_got[0, zz].astype(jnp.float32)
-
-            z_send[zz] = mine[i].astype(jnp.bfloat16)
-            up(zz).start()
+                up(zz, k).wait_recv()
+                add(p, k, z_got, 0, zz)
+
+            send(up)
 
         @pl.when(zz < z)
         def _():
             @pl.when(z < DEPTH - 1)
             def _():
-                down(zz).wait_recv()
-                mine[i] += z_got[1, zz].astype(jnp.float32)
-
-            z_send[zz] = mine[i].astype(jnp.bfloat16)
-            down(zz).start()
-
+                down(zz, k).wait_recv()
+                add(p, k, z_got, 1, zz)
+
+            send(down)
+
+    def close(k):
+        p = 2 * DEPTH - 2 + (0 if k == 3 else 1)
+
+        @pl.when(z > 0)
+        def _():
+            up(z, k).wait_recv()
+            add(p, k, z_got, 0, z)
+
+        @pl.when(z < DEPTH - 1)
+        def _():
+            down(z, k).wait_recv()
+            add(p, k, z_got, 1, z)
+
+    def heads(i):
+        pass_on(i, 3)
+        pass_on(i, 0)
+
+    def tails(i):
+        for k in (1, 2):
+            over(i, k).wait_recv()
+            add(2 * i + 1, k, y_got, i)
+            pass_on(i, k)
+
+    blocks(0)
+    blocks(1)
+    heads(0)
+    blocks(2)
+    heads(1)
+    tails(0)
+    blocks(3)
+    heads(2)
+    tails(1)
+    tails(2)
     last = DEPTH - 1
-    over(last).wait_recv()
-    mine[last] += y_got[last].astype(jnp.float32)
-
-    @pl.when(z > 0)
-    def _():
-        up(z).wait_recv()
-        mine[last] += z_got[0, z].astype(jnp.float32)
-
-    @pl.when(z < DEPTH - 1)
-    def _():
-        down(z).wait_recv()
-        mine[last] += z_got[1, z].astype(jnp.float32)
-
-    out_ref[...] = mine[last]
+    close(3)
+    y_send[last, parts[0], :] = mine[2 * last, parts[0], :].astype(jnp.bfloat16)
+    over(last, 0).start()
+    close(0)
+    x_copy.wait()
+    for k in (1, 2, 0):
+        over(last, k).wait_recv()
+        add(2 * last + 1, k, y_got, last)
+        if k > 0:
+            close(k)
+        total = x[parts[k], :].astype(jnp.float32) + mine[2 * last + 1, parts[k], :]
+        out_ref[parts[k], :] = total.astype(jnp.bfloat16)
     for i in range(DEPTH):
-        over(i).wait_send()
+        over(i, 1).wait_send()
+        over(i, 2).wait_send()
         aside(2 * i).wait_send()
         aside(2 * i + 1).wait_send()
-    for i in range(DEPTH - 1):
-        up(order[i]).wait_send()
-
-
-def output_call(att, pick, wo, members, width):
-    rows = pick.shape[0]
+    over(last, 0).wait_send()
+    for i in range(last):
+        for k in range(4):
+            up(order[i], k).wait_send()
+
+
+def output_call(att, x, wo, members):
+    rows, width = x.shape
     depth = wo.shape[0]
     vmem = pl.BlockSpec(memory_space=pltpu.VMEM)
     dma = pltpu.SemaphoreType.DMA
+    hbm = pl.BlockSpec(memory_space=pl.ANY)
     block = (rows, width)
+    tall = (rows + FIRST, width)
     return pl.pallas_call(
         output_kernel,
-        out_shape=jax.ShapeDtypeStruct(block, jnp.float32),
-        in_specs=[vmem, vmem, pl.BlockSpec(memory_space=pl.ANY)],
+        out_shape=jax.ShapeDtypeStruct(block, jnp.bfloat16),
+        in_specs=[vmem, hbm, hbm],
         out_specs=vmem,
         scratch_shapes=[
             pltpu.VMEM(att.shape, jnp.bfloat16),
             pltpu.VMEM((rows, depth), jnp.bfloat16),
             pltpu.VMEM((members, depth, width), jnp.bfloat16),
-            pltpu.VMEM((DEPTH,) + block, jnp.float32),
+            pltpu.VMEM((2 * DEPTH,) + block, jnp.float32),
             pltpu.VMEM((2 * DEPTH,) + block, jnp.bfloat16),
             pltpu.VMEM((2 * DEPTH,) + block, jnp.bfloat16),
             pltpu.VMEM((DEPTH,) + block, jnp.bfloat16),
             pltpu.VMEM((DEPTH,) + block, jnp.bfloat16),
-            pltpu.VMEM((DEPTH,) + block, jnp.bfloat16),
-            pltpu.VMEM((2, DEPTH) + block, jnp.bfloat16),
+            pltpu.VMEM((DEPTH,) + tall, jnp.bfloat16),
+            pltpu.VMEM((2, DEPTH) + tall, jnp.bfloat16),
+            pltpu.VMEM(block, jnp.bfloat16),
             dma((members,)),
+            dma,
             dma((2, members)),
             dma((2, 2 * DEPTH)),
-            dma((2, DEPTH)),
-            dma((3, DEPTH)),
+            dma((2, DEPTH, 3)),
+            dma((3, DEPTH, 4)),
         ],
         compiler_params=pltpu.CompilerParams(
             collective_id=1, has_side_effects=True, vmem_limit_bytes=56 * 1024 * 1024
         ),
-    )(att, pick, wo)
+    )(att, x, wo)
 
 
 def attention(query3, new_entry, cache_entries, cache_lengths):
@@ -562,25 +679,20 @@
     sums = jnp.pad(sums, ((0, 0), (0, 256 - rows_all))).reshape(4, 128)
     note = jnp.concatenate([sums, norm_gain.reshape(-1, 128)], axis=0)
     note = jnp.pad(note, ((0, -note.shape[0] % 8), (0, 0)))
-    padded = jnp.arange(members * PAD)
-    source = jnp.where(padded % PAD < rows, padded // PAD * rows + padded % PAD, -1)
-    select = (source[:, None] == jnp.arange(rows_all)[None, :]).astype(jnp.bfloat16)
-    pick = (source[None, :] == jnp.arange(rows_all)[:, None]).astype(jnp.bfloat16)
     q_rows, kv_rows = query_call(
-        hidden_state, note, query_weight, keyval_weight, select, members, head_size ** (-0.5)
+        hidden_state, note, query_weight, keyval_weight, members, head_size ** (-0.5)
     )
     query3 = q_rows[:, :rows].transpose(1, 0, 2).reshape(rows, -1, head_size)
     mixed = attention(query3, kv_rows[:rows], cache_entries, cache_lengths)
     att = mixed.reshape(rows, members, cols).transpose(1, 0, 2)
     att = jnp.pad(att, ((0, 0), (0, PAD - rows), (0, 0)))
-    summed = output_call(att, pick, out_weight, members, width)
-    return (hidden_state.astype(jnp.float32) + summed).astype(jnp.bfloat16)
+    return output_call(att, hidden_state, out_weight, members)
 
 
 def on_device(hidden_state, *others):
     members = lax.axis_size("gx")
     rows_all, width = hidden_state.shape
-    fits = width % 128 == 0 and 128 < rows_all <= 256 and rows_all % 16 == 0
+    fits = width % 128 == 0 and 128 < rows_all <= 256 and rows_all % 32 == 0
     if members == 4 * DEPTH and fits and rows_all // members <= PAD:
         return fast_device(hidden_state, *others)
     return plain_device(hidden_state, *others)

time: 127 us -> 117 us (0.921)
  Pallas kernels: 112 us -> 102 us
  other arithmetic: 5.57 us -> 2.9 us
  local copies, waits for them, and re-layouts: 3.33 us -> 5.09 us
    pallas_call x1, Pallas kernels: 54.8 us -> 48.1 us  [output_call(): pl.pallas_call(output_kernel, out_shape=jax.ShapeDtypeStruct(block, jnp.b...]
    pallas_call x1, Pallas kernels: 57.6 us -> 54.3 us  [query_call(): pl.pallas_call(lambda *refs: query_kernel(head_scale, *refs), out_shape=(...]
    convert_element_type x3 -> x0, other arithmetic: 2.66 us -> none  [the longest x1 1.92 us: fast_device(): return (hidden_state.astype(jnp.float32) + summed).astype(jnp.bfloat16)]
    unnamed x6 -> x5, local copies, waits for them, and re-layouts: 2.26 us -> 4.01 us
where the time goes in v2:
time: 117 us; the launch traced here: 116 us
  Pallas kernels  102 us (87%)
  matrix products  5.2 us (4%)
  local copies, waits for them, and re-layouts  5.09 us (4%)
  other arithmetic  2.9 us (2%)
    pallas_call x1, Pallas kernels, query_call(): pl.pallas_call(lambda *refs: query_kernel(head_scale, *refs), out_shape=(...  54.3 us
    pallas_call x1, Pallas kernels, output_call(): pl.pallas_call(output_kernel, out_shape=jax.ShapeDtypeStruct(block, jnp.b...  48.1 us
    unnamed x5, local copies, waits for them, and re-layouts  4.01 us
    dot_general x1, matrix products, attention(): jnp.einsum('rhd,rld->rhl', query3, keys, preferred_element_type=jnp.float32)  2.71 us
    dot_general x1, matrix products, attention(): jnp.einsum('rhl,rld->rhd', probs, values, preferred_element_type=jnp.floa...  2.36 us

profile of v2, /device:TPU:0, one launch (start us, length us, event | category | flops | bytes accessed | tf_op | source)
XLA Modules:
  0.0 115.7 jit_solution(1567803788682593375)
XLA Ops:
  0.0 1.2 %convert_reduce_fusion = (f32[160]{0:T(256)S(1)}, f32[160]{0:T(256)S(1)}) fusion(bf16[160,1152]{1,0:T(8,128)(2,1)} %x_hbm.1), kind=kLoop, calls=%fused_computation.8 | loop fusion | flops 736960 | bytes 369920 | tf_op jit(solution)/shard_map/reduce_sum | solution.py:678
  1.2 0.7 select_maximum_fusion.refs_1_
  1.9 0.7 fusion.23
  2.6 0.0 copy-start
  2.6 1.0 copy-done
  3.6 0.0 copy-start.1
  3.6 1.3 %copy-done.1 = bf16[1152,512]{1,0:T(8,128)(2,1)S(1)} copy-done((bf16[1152,512]{1,0:T(8,128)(2,1)S(1)}, bf16[1152,512]{1,0:T(8,128)(2,1)}, u32[]{:S(2)}) %copy-start.1) | copy-done | bytes 1179672
  4.9 54.3 %shard_map.73 = (bf16[16,16,512]{2,1,0:T(8,128)(2,1)S(1)}, bf16[16,512]{1,0:T(8,128)(2,1)S(1)}) custom-call(bf16[160,1152]{1,0:T(8,128)(2,1)S(1)} %copy-done, f32[16,128]{1,0:T(8,128)S(1)} %select_maximum_fusion.refs_1_, bf16[18432,512]{1,0:T(8,128)(2,1)} %refs_2_.1, bf16[1152,512]{1,0:T(8,128)(2,1)S(1)} %copy-done.1), custom_call_target="tpu_custom_call" | custom-call | tf_op jit(solution)/shard_map/pallas_call | solution.py:355
  59.2 0.1 copy.8
  59.3 0.1 reshape.51
  59.4 0.1 fusion.18
  59.6 2.7 %fusion.24 = (f32[10,32]{1,0:T(8,128)S(1)}, f32[10,32,512]{2,1,0:T(8,128)S(1)}) fusion(bf16[10,32,256]{2,1,0:T(8,128)(2,1)S(1)} %reshape.51, bf16[10,512,512]{2,1,0:T(8,128)(2,1)} %param.12, pred[10,512]{1,0:T(8,128)(4,1)S(1)} %get-tuple-element.16), kind=kOutput, calls=%fused_computation.33 | convolution fusion | flops 84213440 | bytes 3447040 | tf_op jit(solution)/shard_map/rhd,rld->rhl/dot_general | solution.py:650
  62.3 0.3 fusion.14
  62.6 2.4 %fusion.10 = bf16[10,32,256]{2,1,0:T(8,128)(2,1)S(1)} fusion(bf16[10,512,512]{2,1,0:T(8,128)(2,1)} %param.12, f32[10,32,512]{2,1,0:T(8,128)S(1)} %get-tuple-element.18, f32[10,32]{1,0:T(8,128)S(1)} %get-tuple-element.12, f32[10,512]{1,0:T(8,128)S(1)} %get-tuple-element.15, f32[10,32]{1,0:T(8,128)S(1)} %bitcast_maximum_fusion, ...), kind=kOutput, calls=%fused_computation.6 | convolution fusion | flops 84787200 | bytes 3475200 | tf_op jit(solution)/shard_map/rhl,rld->rhd/dot_general | solution.py:662
  64.9 0.1 reshape.52
  65.0 0.1 copy.31
  65.1 0.7 pad.14.att_ref
  65.8 48.1 %shard_map.74 = bf16[160,1152]{1,0:T(8,128)(2,1)} custom-call(bf16[16,16,512]{2,1,0:T(8,128)(2,1)} %pad.14.att_ref, bf16[160,1152]{1,0:T(8,128)(2,1)} %x_hbm.1, bf16[512,18432]{1,0:T(8,128)(2,1)} %wo_hbm.1), custom_call_target="tpu_custom_call" | custom-call | tf_op jit(solution)/shard_map/pallas_call | solution.py:616
  114.0 1.8 %copy.33 = bf16[160,1152]{1,0:T(8,128)(2,1)} copy(bf16[160,1152]{1,0:T(8,128)(2,1)} %shard_map.74) | data formatting | bytes 737280
  (6 shorter events, 0.1 us)
Async XLA Ops:
  2.6 1.0 copy-start
  3.6 1.3 %copy-start.1 = (bf16[1152,512]{1,0:T(8,128)(2,1)S(1)}, bf16[1152,512]{1,0:T(8,128)(2,1)}, u32[]{:S(2)}) copy-start(bf16[1152,512]{1,0:T(8,128)(2,1)} %refs_3_.1) | copy-start | bytes 3538948

commit v3 on v2

--- a/solution.py
+++ b/solution.py
@@ -129,12 +129,15 @@
     note_ref,
     wq_hbm,
     kvw_hbm,
-    q_out,
-    kv_out,
+    cache_hbm,
+    lengths,
+    att_out,
     buf,
     notes,
     wbuf,
     kvw,
+    cache,
+    att_rows,
     acc,
     stat,
     q_send,
@@ -171,6 +174,7 @@
     own.start()
     kvw_copy = pltpu.make_async_copy(kvw_hbm, kvw, own_sem.at[1])
     kvw_copy.start()
+    cache_copy = pltpu.make_async_copy(cache_hbm, cache, own_sem.at[2])
     notes[me] = note_ref[...]
     order = far_to_near(z)[::-1]
     own.wait()
@@ -248,6 +252,7 @@
     aside(z, y).start()
     for slot in range(members):
         weights_copy(slot).start()
+    cache_copy.start()
     collect(lambda peer: note_ref, notes, note_sem)
 
     mean = jnp.sum(notes[:, 0:2, :], axis=0) / total_width
@@ -318,7 +323,9 @@
     spread(lambda peer: q_send.at[peer], q_got, q_sem)
     q_got[me] = q_send[me]
     collect(lambda peer: kv_send.at[peer], kv_got, kv_sem)
-    kv_out[...] = jnp.sum(kv_got[...].astype(jnp.float32), axis=0).astype(jnp.bfloat16)
+    fresh_kv = jnp.sum(kv_got[...].astype(jnp.float32), axis=0).astype(jnp.bfloat16)
+    fresh_kv = fresh_kv.astype(jnp.float32)
+    cache_copy.wait()
     for zz in range(DEPTH):
         for piece in range(3):
             over_sent = (piece > 0) | (zz == z)
@@ -341,10 +348,44 @@
                 down(zz, piece).wait_send()
 
     collect(lambda peer: q_send.at[peer], q_got, q_sem)
-    q_out[...] = q_got[...]
-
-
-def query_call(x, note, wq, kvw, members, head_scale):
+    shape = (members * PAD, members * PAD)
+    to = lax.broadcasted_iota(jnp.int32, shape, 0)
+    of = lax.broadcasted_iota(jnp.int32, shape, 1)
+    turn = ((to & (PAD - 1)) * PAD + (to >> 4)) == of
+    turn = jnp.where(turn, 1.0, 0.0).astype(jnp.bfloat16)
+    flat = q_got[...].reshape(members * PAD, q_got.shape[2])
+    by_row = jnp.dot(turn, flat, preferred_element_type=jnp.float32)
+    local = rows // members
+    head = cache.shape[2] // 2
+    att_rows[...] = jnp.zeros_like(att_rows)
+    for r in range(local):
+        span = slice(r * PAD, (r + 1) * PAD)
+        q32 = jnp.concatenate([by_row[span, 0:head], by_row[span, head : 2 * head]], axis=0)
+        scores = lax.dot_general(
+            q32.astype(jnp.bfloat16),
+            cache[r, :, 0:head],
+            (((1,), (1,)), ((), ())),
+            preferred_element_type=jnp.float32,
+        )
+        fresh = jnp.sum(q32 * fresh_kv[r : r + 1, 0:head], axis=1, keepdims=True)
+        slots = lax.broadcasted_iota(jnp.int32, scores.shape, 1)
+        valid = slots < lengths[r]
+        scores = jnp.where(valid, scores, -1e30)
+        peak = jnp.maximum(jnp.max(scores, axis=1, keepdims=True), fresh)
+        weights = jnp.where(valid, jnp.exp(scores - peak), 0.0)
+        fresh_w = jnp.exp(fresh - peak)
+        total = jnp.sum(weights, axis=1, keepdims=True) + fresh_w
+        probs = (weights / total).astype(jnp.bfloat16)
+        fresh_p = (fresh_w / total).astype(jnp.bfloat16).astype(jnp.float32)
+        mixed = jnp.dot(probs, cache[r, :, head : 2 * head], preferred_element_type=jnp.float32)
+        mixed = (mixed + fresh_p * fresh_kv[r : r + 1, head : 2 * head]).astype(jnp.bfloat16)
+        att_rows[span, 0:head] = mixed[0:PAD]
+        att_rows[span, head : 2 * head] = mixed[PAD : 2 * PAD]
+    back = jnp.dot(turn, att_rows[...], preferred_element_type=jnp.float32)
+    att_out[...] = back.astype(jnp.bfloat16).reshape(att_out.shape)
+
+
+def query_call(x, note, wq, kvw, cache, lengths, members, head_scale):
     rows, width = x.shape
     cols = wq.shape[1]
     vmem = pl.BlockSpec(memory_space=pltpu.VMEM)
@@ -354,17 +395,16 @@
     dma = pltpu.SemaphoreType.DMA
     return pl.pallas_call(
         lambda *refs: query_kernel(head_scale, *refs),
-        out_shape=(
-            jax.ShapeDtypeStruct(swap, jnp.bfloat16),
-            jax.ShapeDtypeStruct((PAD, kv_cols), jnp.bfloat16),
-        ),
-        in_specs=[hbm, vmem, hbm, hbm],
-        out_specs=(vmem, vmem),
+        out_shape=jax.ShapeDtypeStruct(swap, jnp.bfloat16),
+        in_specs=[hbm, vmem, hbm, hbm, hbm, pl.BlockSpec(memory_space=pltpu.SMEM)],
+        out_specs=vmem,
         scratch_shapes=[
             pltpu.VMEM((members, rows, width), jnp.bfloat16),
             pltpu.VMEM((members,) + note.shape, jnp.float32),
             pltpu.VMEM((members, width, cols), jnp.bfloat16),
             pltpu.VMEM(kvw.shape, jnp.bfloat16),
+            pltpu.VMEM(cache.shape, jnp.bfloat16),
+            pltpu.VMEM((members * PAD, cols), jnp.bfloat16),
             pltpu.VMEM((rows, cols), jnp.float32),
             pltpu.VMEM((2, rows, 128), jnp.float32),
             pltpu.VMEM(swap, jnp.bfloat16),
@@ -372,7 +412,7 @@
             pltpu.VMEM((members, PAD, kv_cols), jnp.bfloat16),
             pltpu.VMEM((members, PAD, kv_cols), jnp.bfloat16),
             dma((members,)),
-            dma((2,)),
+            dma((3,)),
             dma((2, DEPTH, 4)),
             dma((DEPTH, 3)),
             dma((2 * DEPTH,)),
@@ -382,9 +422,9 @@
             dma((2, members)),
         ],
         compiler_params=pltpu.CompilerParams(
-            collective_id=0, has_side_effects=True, vmem_limit_bytes=48 * 1024 * 1024
+            collective_id=0, has_side_effects=True, vmem_limit_bytes=60 * 1024 * 1024
         ),
-    )(x, note, wq, kvw)
+    )(x, note, wq, kvw, cache, lengths)
 
 
 def output_kernel(
@@ -638,32 +678,9 @@
             dma((3, DEPTH, 4)),
         ],
         compiler_params=pltpu.CompilerParams(
-            collective_id=1, has_side_effects=True, vmem_limit_bytes=56 * 1024 * 1024
+            collective_id=1, has_side_effects=True, vmem_limit_bytes=60 * 1024 * 1024
         ),
     )(att, x, wo)
-
-
-def attention(query3, new_entry, cache_entries, cache_lengths):
-    head_size = query3.shape[2]
-    keys = cache_entries[:, :, :head_size]
-    values = cache_entries[:, :, head_size:]
-    scores = jnp.einsum("rhd,rld->rhl", query3, keys, preferred_element_type=jnp.float32)
-    fresh = jnp.einsum(
-        "rhd,rd->rh", query3, new_entry[:, :head_size], preferred_element_type=jnp.float32
-    )
-    valid = jnp.arange(keys.shape[1])[None, :] < cache_lengths[:, None]
-    scores = jnp.where(valid[:, None, :], scores, -1e30)
-    peak = jnp.maximum(jnp.max(scores, axis=-1), fresh)
-    weights = jnp.exp(scores - peak[..., None]) * valid[:, None, :].astype(jnp.float32)
-    fresh_w = jnp.exp(fresh - peak)
-    total = jnp.sum(weights, axis=-1) + fresh_w
-    probs = (weights / total[..., None]).astype(jnp.bfloat16)
-    fresh_p = (fresh_w / total).astype(jnp.bfloat16)
-    mixed = jnp.einsum("rhl,rld->rhd", probs, values, preferred_element_type=jnp.float32)
-    mixed = mixed + fresh_p.astype(jnp.float32)[..., None] * new_entry[:, None, head_size:].astype(
-        jnp.float32
-    )
-    return mixed.astype(jnp.bfloat16)
 
 
 def fast_device(
@@ -671,21 +688,22 @@
 ):
     members = lax.axis_size("gx")
     rows_all, width = hidden_state.shape
-    rows = rows_all // members
     head_size = keyval_weight.shape[1] // 2
-    cols = query_weight.shape[1]
     state32 = hidden_state.astype(jnp.float32)
     sums = jnp.stack([jnp.sum(state32, axis=1), jnp.sum(state32 * state32, axis=1)])
     sums = jnp.pad(sums, ((0, 0), (0, 256 - rows_all))).reshape(4, 128)
     note = jnp.concatenate([sums, norm_gain.reshape(-1, 128)], axis=0)
     note = jnp.pad(note, ((0, -note.shape[0] % 8), (0, 0)))
-    q_rows, kv_rows = query_call(
-        hidden_state, note, query_weight, keyval_weight, members, head_size ** (-0.5)
-    )
-    query3 = q_rows[:, :rows].transpose(1, 0, 2).reshape(rows, -1, head_size)
-    mixed = attention(query3, kv_rows[:rows], cache_entries, cache_lengths)
-    att = mixed.reshape(rows, members, cols).transpose(1, 0, 2)
-    att = jnp.pad(att, ((0, 0), (0, PAD - rows), (0, 0)))
+    att = query_call(
+        hidden_state,
+        note,
+        query_weight,
+        keyval_weight,
+        cache_entries,
+        cache_lengths,
+        members,
+        head_size ** (-0.5),
+    )
     return output_call(att, hidden_state, out_weight, members)
 
 
@@ -693,7 +711,8 @@
     members = lax.axis_size("gx")
     rows_all, width = hidden_state.shape
     fits = width % 128 == 0 and 128 < rows_all <= 256 and rows_all % 32 == 0
-    if members == 4 * DEPTH and fits and rows_all // members <= PAD:
+    paired = others[1].shape[1] == others[2].shape[1] and members == PAD
+    if members == 4 * DEPTH and fits and paired and rows_all // members <= PAD:
         return fast_device(hidden_state, *others)
     return plain_device(hidden_state, *others)
 

time: 117 us -> 115 us (0.983)
  Pallas kernels: 102 us -> 109 us
  matrix products: 5.2 us -> 0 us
  local copies, waits for them, and re-layouts: 5.09 us -> 1.77 us
    pallas_call x1, Pallas kernels: 54.3 us -> 60.6 us  [query_call(): pl.pallas_call(lambda *refs: query_kernel(head_scale, *refs), out_shape=j...]
    dot_general x3 -> x0, matrix products: 5.2 us -> none  [the longest x1 2.71 us: attention(): jnp.einsum('rhd,rld->rhl', query3, keys, preferred_element_type=jnp.float32)]
    unnamed x5 -> x1, local copies, waits for them, and re-layouts: 4.01 us -> 1.75 us
where the time goes in v3:
time: 115 us; the launch traced here: 113 us
  Pallas kernels  109 us (95%)
  other arithmetic  2.48 us (2%)
  local copies, waits for them, and re-layouts  1.77 us (2%)
    pallas_call x1, Pallas kernels, query_call(): pl.pallas_call(lambda *refs: query_kernel(head_scale, *refs), out_shape=j...  60.6 us
    pallas_call x1, Pallas kernels, output_call(): pl.pallas_call(output_kernel, out_shape=jax.ShapeDtypeStruct(block, jnp.b...  48.2 us

profile of v3, /device:TPU:0, one launch (start us, length us, event | category | flops | bytes accessed | tf_op | source)
XLA Modules:
  0.0 113.1 jit_solution(14716455541205468434)
XLA Ops:
  0.0 1.2 %convert_reduce_fusion = (f32[160]{0:T(256)S(1)}, f32[160]{0:T(256)S(1)}) fusion(bf16[160,1152]{1,0:T(8,128)(2,1)} %x_hbm.1), kind=kLoop, calls=%fused_computation.1 | loop fusion | flops 736960 | bytes 369920 | tf_op jit(solution)/shard_map/reduce_sum | solution.py:693
  1.2 1.3 %select_maximum_fusion.refs_1_ = f32[16,128]{1,0:T(8,128)} fusion(f32[9,128]{1,0:T(8,128)} %bitcast.3, f32[4,128]{1,0:T(4,128)S(1)} %reshape.6), kind=kLoop, calls=%fused_computation.3 | loop fusion | flops 8192 | bytes 14848 | tf_op jit(solution)/shard_map/concatenate | solution.py:695
  2.5 60.6 %shard_map.73.att_ref = bf16[16,16,512]{2,1,0:T(8,128)(2,1)} custom-call(bf16[160,1152]{1,0:T(8,128)(2,1)} %x_hbm.1, f32[16,128]{1,0:T(8,128)} %select_maximum_fusion.refs_1_, bf16[18432,512]{1,0:T(8,128)(2,1)} %refs_2_.1, bf16[1152,512]{1,0:T(8,128)(2,1)} %refs_3_.1, bf16[10,512,512]{2,1,0:T(8,128)(2,1)} %refs_4_.1, s32[10]{0:T(128)} %refs_5_.1), custom_call_target="tpu_custom_call" | custom-call | tf_op jit(solution)/shard_map/pallas_call | solution.py:396
  63.1 48.2 %shard_map.74 = bf16[160,1152]{1,0:T(8,128)(2,1)} custom-call(bf16[16,16,512]{2,1,0:T(8,128)(2,1)} %shard_map.73.att_ref, bf16[160,1152]{1,0:T(8,128)(2,1)} %x_hbm.1, bf16[512,18432]{1,0:T(8,128)(2,1)} %wo_hbm.1), custom_call_target="tpu_custom_call" | custom-call | tf_op jit(solution)/shard_map/pallas_call | solution.py:656
  111.4 1.8 %copy.9 = bf16[160,1152]{1,0:T(8,128)(2,1)} copy(bf16[160,1152]{1,0:T(8,128)(2,1)} %shard_map.74) | data formatting | bytes 737280
  (2 shorter events, 0.0 us)

commit v4 on v3

--- a/solution.py
+++ b/solution.py
@@ -144,6 +144,7 @@
     q_got,
     kv_send,
     kv_got,
+    kv_pair,
     w_sem,
     own_sem,
     z_sem,
@@ -153,6 +154,7 @@
     note_sem,
     kv_sem,
     q_sem,
+    pair_sem,
 ):
     members = buf.shape[0]
     rows, width = x_hbm.shape
@@ -278,8 +280,27 @@
     kv = jnp.dot(normed(me), kvw[...], preferred_element_type=jnp.float32)
     kv = jnp.dot(select, kv.astype(jnp.bfloat16), preferred_element_type=jnp.float32)
     kv_send[...] = kv.astype(jnp.bfloat16).reshape(kv_send.shape)
-    spread(lambda peer: kv_send.at[peer], kv_got, kv_sem)
-    kv_got[me] = kv_send[me]
+
+    def to_pair(k, theirs):
+        return remote(
+            kv_send.at[2 * k + theirs], kv_pair.at[k], pair_sem.at[0, k], pair_sem.at[1, k], sibling
+        )
+
+    def to_owner(k, slot):
+        peer = (me + 2 * k) % members
+        return remote(
+            kv_send.at[peer], kv_got.at[slot], kv_sem.at[0, peer], kv_sem.at[1, slot], peer
+        )
+
+    for k in range(members // 2):
+        to_pair(k, 1 - c).start()
+    for k in range(members // 2):
+        to_pair(k, 1 - c).wait()
+        pair = kv_send[2 * k + c].astype(jnp.float32) + kv_pair[k].astype(jnp.float32)
+        kv_send[2 * k + c] = pair.astype(jnp.bfloat16)
+    for k in range(1, members // 2):
+        to_owner(k, me // 2).start()
+    kv_got[me // 2] = kv_send[me]
     acc[...] = jnp.zeros_like(acc)
 
     def work(zz, yy):
@@ -322,7 +343,8 @@
     q_send[...] = query.astype(jnp.bfloat16).reshape(q_send.shape)
     spread(lambda peer: q_send.at[peer], q_got, q_sem)
     q_got[me] = q_send[me]
-    collect(lambda peer: kv_send.at[peer], kv_got, kv_sem)
+    for k in range(1, members // 2):
+        to_owner(k, (me + 2 * k) % members // 2).wait()
     fresh_kv = jnp.sum(kv_got[...].astype(jnp.float32), axis=0).astype(jnp.bfloat16)
     fresh_kv = fresh_kv.astype(jnp.float32)
     cache_copy.wait()
@@ -410,7 +432,8 @@
             pltpu.VMEM(swap, jnp.bfloat16),
             pltpu.VMEM(swap, jnp.bfloat16),
             pltpu.VMEM((members, PAD, kv_cols), jnp.bfloat16),
-            pltpu.VMEM((members, PAD, kv_cols), jnp.bfloat16),
+            pltpu.VMEM((members // 2, PAD, kv_cols), jnp.bfloat16),
+            pltpu.VMEM((members // 2, PAD, kv_cols), jnp.bfloat16),
             dma((members,)),
             dma((3,)),
             dma((2, DEPTH, 4)),
@@ -420,6 +443,7 @@
             dma((2, members)),
             dma((2, members)),
             dma((2, members)),
+            dma((2, members // 2)),
         ],
         compiler_params=pltpu.CompilerParams(
             collective_id=0, has_side_effects=True, vmem_limit_bytes=60 * 1024 * 1024

time: 115 us -> 113 us (0.983)
  Pallas kernels: 109 us -> 107 us
    pallas_call x1, Pallas kernels: 60.6 us -> 57.9 us  [query_call(): pl.pallas_call(lambda *refs: query_kernel(head_scale, *refs), out_shape=j...]
where the time goes in v4:
time: 113 us; the launch traced here: 111 us
  Pallas kernels  107 us (95%)
  other arithmetic  2.48 us (2%)
  local copies, waits for them, and re-layouts  1.77 us (2%)
    pallas_call x1, Pallas kernels, query_call(): pl.pallas_call(lambda *refs: query_kernel(head_scale, *refs), out_shape=j...  57.9 us
    pallas_call x1, Pallas kernels, output_call(): pl.pallas_call(output_kernel, out_shape=jax.ShapeDtypeStruct(block, jnp.b...  48.7 us

profile of v4, /device:TPU:0, one launch (start us, length us, event | category | flops | bytes accessed | tf_op | source)
XLA Modules:
  0.0 110.8 jit_solution(12688016331466118011)
XLA Ops:
  0.0 1.2 %convert_reduce_fusion = (f32[160]{0:T(256)S(1)}, f32[160]{0:T(256)S(1)}) fusion(bf16[160,1152]{1,0:T(8,128)(2,1)} %x_hbm.1), kind=kLoop, calls=%fused_computation.1 | loop fusion | flops 736960 | bytes 369920 | tf_op jit(solution)/shard_map/reduce_sum | solution.py:717
  1.2 1.3 %select_maximum_fusion.refs_1_ = f32[16,128]{1,0:T(8,128)} fusion(f32[9,128]{1,0:T(8,128)} %bitcast.3, f32[4,128]{1,0:T(4,128)S(1)} %reshape.6), kind=kLoop, calls=%fused_computation.3 | loop fusion | flops 8192 | bytes 14848 | tf_op jit(solution)/shard_map/concatenate | solution.py:719
  2.5 57.9 %shard_map.73.att_ref = bf16[16,16,512]{2,1,0:T(8,128)(2,1)} custom-call(bf16[160,1152]{1,0:T(8,128)(2,1)} %x_hbm.1, f32[16,128]{1,0:T(8,128)} %select_maximum_fusion.refs_1_, bf16[18432,512]{1,0:T(8,128)(2,1)} %refs_2_.1, bf16[1152,512]{1,0:T(8,128)(2,1)} %refs_3_.1, bf16[10,512,512]{2,1,0:T(8,128)(2,1)} %refs_4_.1, s32[10]{0:T(128)} %refs_5_.1), custom_call_target="tpu_custom_call" | custom-call | tf_op jit(solution)/shard_map/pallas_call | solution.py:418
  60.4 48.7 %shard_map.74 = bf16[160,1152]{1,0:T(8,128)(2,1)} custom-call(bf16[16,16,512]{2,1,0:T(8,128)(2,1)} %shard_map.73.att_ref, bf16[160,1152]{1,0:T(8,128)(2,1)} %x_hbm.1, bf16[512,18432]{1,0:T(8,128)(2,1)} %wo_hbm.1), custom_call_target="tpu_custom_call" | custom-call | tf_op jit(solution)/shard_map/pallas_call | solution.py:680
  109.1 1.8 %copy.9 = bf16[160,1152]{1,0:T(8,128)(2,1)} copy(bf16[160,1152]{1,0:T(8,128)(2,1)} %shard_map.74) | data formatting | bytes 737280
  (2 shorter events, 0.0 us)
